TPU v7x, 256 devices: a whole 4x4x8 slice. The times are simulated.
256 devices in a mesh: row: 16 (over z, core), col: 16 (over x, y).
Axes of the slice: x: 4, y: 4, z: 8, core: 2. Of those that a mesh axis runs over, the one named last changes fastest.
Arguments:
- matrix: float32 [4, 16, 128, 4, 16, 128], P(None, 'row', None, None, 'col'), may hold values from 0 to 3.5, as said below
Outputs:
- factored: float32 [4, 16, 128, 4, 16, 128], P(None, 'row', None, None, 'col')
Inputs may be any that keep to these rules, and one draw needn't show every extreme that they name: matrix is symmetric, and its smallest eigenvalue is at least 0.5.
All inputs are finite; a program needn't handle non-finite values.
Results may differ from a plain program's by a relative error of at most 0.00016.
Values sent between devices are 32-bit elements; how exact they have to be, the bound alone decides.
A program may use at most 64 MiB of HBM per device.

v0:
```python
import functools

import jax
import jax.numpy as jnp
from jax import lax
from jax.experimental import pallas as pl
from jax.experimental.pallas import tpu as pltpu
from jax.sharding import PartitionSpec as P

F32 = jnp.float32
MESH = pl.DeviceIdType.MESH
HIGHEST = lax.Precision.HIGHEST
NB = 128
LOOK = 2
CHUNK = 64
CHUNKS = 512 // CHUNK


def dot_nn(a, b):
    return jnp.dot(a, b, precision=HIGHEST, preferred_element_type=F32)


def dot_nt(a, b):
    return lax.dot_general(
        a, b, (((1,), (1,)), ((), ())), precision=HIGHEST, preferred_element_type=F32
    )


def row_splat(tile, k):
    return jnp.broadcast_to(tile[k : k + 1, :], (8, NB))


def lane_splat(tile, k):
    return jnp.broadcast_to(tile[:, k : k + 1], (8, NB))


def eliminate(rows, rows_identity, columns):
    sub = lax.broadcasted_iota(jnp.int32, (8, NB), 0)
    columns = list(columns)
    upper, inverse, solved = rows, rows_identity, rows_identity
    scale = jnp.ones((8, NB), F32)
    for k in range(8):
        pivot = row_splat(columns[k], k)
        over = 1.0 / pivot
        here = sub == k
        ratio = columns[k] * over
        below = jnp.where(sub > k, ratio, 0.0)
        for j in range(k + 1, 8):
            r = row_splat(columns[j], k)
            columns[j] = jnp.where(here, r * over, columns[j] - ratio * r)
        upper = upper - below * row_splat(upper, k)
        inverse = inverse - below * row_splat(inverse, k)
        r = row_splat(solved, k)
        solved = jnp.where(here, r * over, solved - ratio * r)
        scale = jnp.where(here, lax.rsqrt(pivot), scale)
    return upper * scale, inverse * scale, solved


def factor(work, solved_rows, upper, inverse):
    lane = lax.broadcasted_iota(jnp.int32, (8, NB), 1)
    sub = lax.broadcasted_iota(jnp.int32, (8, NB), 0)
    solved_rows[...] = jnp.zeros((NB, NB), F32)
    steps = NB // 8
    for t in range(steps):
        o = 8 * t
        rows = work[o : o + 8, :]
        columns = [lane_splat(rows, o + j) for j in range(8)]
        block = (lane >= o) & (lane < o + 8)
        rows_identity = jnp.where(block, (lane - o == sub).astype(F32), rows)
        up, inv, solved = eliminate(rows, rows_identity, columns)
        upper[o : o + 8, :] = jnp.where(lane >= o, up, 0.0)
        inverse[o : o + 8, :] = jnp.where(lane < o + 8, inv, 0.0)
        solved_rows[o : o + 8, :] = solved
        splats = [row_splat(solved, j) for j in range(8)]
        for i in range(t + 1, min(t + 1 + LOOK, steps)):
            tile = work[8 * i : 8 * i + 8, :]
            total = jnp.where(block, 0.0, tile)
            for j in range(8):
                total = total - lane_splat(tile, o + j) * splats[j]
            work[8 * i : 8 * i + 8, :] = total
        rest = 8 * (t + 1 + LOOK)
        if rest < NB:
            tiles = work[rest:, :]
            lanes = lax.broadcasted_iota(jnp.int32, (NB - rest, NB), 1)
            own = (lanes >= o) & (lanes < o + 8)
            work[rest:, :] = jnp.where(own, 0.0, tiles) - dot_nn(
                jnp.where(own, tiles, 0.0), solved_rows[...]
            )


def gather_kernel(
    n,
    x_hbm,
    pr,
    pc,
    diag,
    xv,
    panel,
    lead,
    rbuf,
    cbuf,
    wbuf,
    wown,
    ac,
    work,
    solved_rows,
    upper,
    inverse,
    w10,
    handed,
    load_sem,
    lead_recv,
    lead_send,
    diag_recv,
    diag_send,
    go_plane,
    go_line,
    go_down,
    hand_recv,
    hand_send,
    hand_rows,
    hand_line,
    r_piece,
    r_gather,
    r_send_a,
    r_send_b,
    c_recv,
    c_send,
    c_pair,
    c_pair_send,
    w_piece,
    w_gather,
    w_send_a,
    w_send_b,
    w_send_c,
):
    r = lax.axis_index("row")
    c = lax.axis_index("col")
    z = r // 2
    core = lax.rem(r, 2)
    pair = r + 1 - 2 * core
    both, either, no = jnp.logical_and, jnp.logical_or, jnp.logical_not
    left = c < 2
    corner = both(r == 0, c == 0)
    last = both(r == 1, c == 1)

    def span(first, end, body):
        def step(k, carry):
            body(k)
            return carry

        lax.fori_loop(first, end, step, 0)

    def each(body):
        span(1, n, body)

    def other(me, k):
        return lax.rem(me + k, n)

    def copy(src, dst, send, recv, row, col):
        return pltpu.make_async_remote_copy(
            src_ref=src,
            dst_ref=dst,
            send_sem=send,
            recv_sem=recv,
            device_id=(row, col),
            device_id_type=MESH,
        )

    def signal(sem, row, col):
        pl.semaphore_signal(sem, inc=1, device_id=(row, col), device_id_type=MESH)

    def arrive(buffer, sem):
        pltpu.make_async_copy(buffer, buffer, sem).wait()

    hub = both(r == 1, c == 0)
    barrier = pltpu.get_barrier_semaphore()
    before = jnp.where(z < 5, r - 2, jnp.where(z < 7, r + 2, r - 2))
    signal(barrier, pair, c)

    @pl.when(z > 0)
    def _():
        signal(barrier, before, c)

    @pl.when(z != 4)
    def _():
        signal(barrier, 8, c)

    @pl.when(either(hub, both(z == 0, c != 0)))
    def _():
        signal(barrier, r + 12, c)

    @pl.when(hub)
    def _():
        signal(barrier, 12, c)

    for k in range(2):

        @pl.when(c != k)
        def _():
            signal(barrier, jnp.where(z > 0, r, 0), k)

    @pl.when(corner)
    def _():
        signal(barrier, 1, 1)

    top = pltpu.make_async_copy(x_hbm.at[pl.ds(0, 512)], xv.at[pl.ds(0, 512)], load_sem.at[0])
    below = pltpu.make_async_copy(
        x_hbm.at[pl.ds(512, 1536)], xv.at[pl.ds(512, 1536)], load_sem.at[1]
    )
    top.start()
    below.start()
    top.wait()

    @pl.when(left)
    def _():
        panel[0:NB, :] = xv[pl.ds(0, NB, stride=4), :]

    def load_rest():
        below.wait()

        @pl.when(left)
        def _():
            panel[NB:, :] = xv[pl.ds(512, 384, stride=4), :]

    def enter():
        after = jnp.where(either(z == 4, z == 5), 0, jnp.where(z == 6, 3, 1))
        heard = (
            1
            + after
            + jnp.where(r == 8, n - 2, 0)
            + jnp.where(both(z > 0, left), n - 1, 0)
            + jnp.where(both(r == 0, left), 2 * (n - 1), 0)
            + jnp.where(last, 1, 0)
        )
        pl.semaphore_wait(barrier, heard)

    def to_corner(b):
        return copy(panel.at[pl.ds(0, NB)], lead.at[b], lead_send, lead_recv.at[b], 0, 0)

    def r_scatter(k):
        p = other(c, k)
        return copy(
            panel.at[pl.ds(pl.multiple_of(p * 32, 32), 32)],
            rbuf.at[p, c],
            r_send_a.at[p],
            r_piece.at[c],
            r,
            p,
        )

    def r_across(k):
        p = other(c, k)
        return copy(rbuf.at[c], rbuf.at[c], r_send_b.at[p], r_gather.at[c], r, p)

    def plane_scatter():
        each(lambda k: r_scatter(k).start())
        rbuf[c, c] = panel[pl.ds(pl.multiple_of(c * 32, 32), 32), :]

    def plane_gather():
        @pl.when(c != 0)
        def _():
            arrive(rbuf.at[c, 0], r_piece.at[0])

        @pl.when(c != 1)
        def _():
            arrive(rbuf.at[c, 1], r_piece.at[1])

        each(lambda k: r_across(k).start())

    def chunk(k):
        return cbuf.at[core, pl.ds(pl.multiple_of(k * CHUNK, CHUNK), CHUNK)]

    def first_chunk(k):
        return xv.at[pl.ds(pl.multiple_of(k * CHUNK, CHUNK), CHUNK)]

    def c_next(k, way, src):
        there = lax.rem(r + 2 + way * (n - 4), n)
        return copy(src, chunk(k), c_send.at[way, k], c_recv.at[k], there, c)

    def c_beside(k, src):
        return copy(src, chunk(k), c_pair_send.at[k], c_pair.at[k], pair, c)

    def line_up(k):
        c_next(k, 0, first_chunk(k)).start()
        c_beside(k, first_chunk(k)).start()

    def line_down(k):
        c_next(k, 1, first_chunk(k)).start()

    up = both(z >= 1, z <= 3)
    down = z >= 6

    def line_relay(k):
        arrive(chunk(k), c_recv.at[k])

        @pl.when(up)
        def _():
            c_next(k, 0, chunk(k)).start()

        @pl.when(down)
        def _():
            c_next(k, 1, chunk(k)).start()

        c_beside(k, chunk(k)).start()

    def w_copy(send, recv, row, col):
        return copy(wbuf.at[c], wbuf.at[c], send, recv, row, col)

    def w_scatter(p):
        return copy(wown.at[p], wbuf.at[p], w_send_a.at[p], w_piece, 1, p)

    def w_down(k):
        p = other(r, k)
        return w_copy(w_send_b.at[p], w_piece, p, c)

    def w_across(k):
        p = other(c, k)
        return w_copy(w_send_c.at[p], w_gather.at[c], r, p)

    def diagonal():
        return copy(upper.at[1], diag, diag_send, diag_recv, 1, 1)

    def pass_w():
        arrive(wbuf.at[c], w_piece)

        @pl.when(r == 1)
        def _():
            pl.semaphore_wait(go_line, 1)
            each(lambda k: w_down(k).start())

        each(lambda k: w_across(k).start())

    def hand(b):
        src = panel if b == 0 else xv.at[pl.ds(0, 512)]
        dst = handed if b == 0 else cbuf.at[0]
        return copy(src, dst, hand_send.at[b], hand_recv.at[b], 1, 0)

    def hand_scatter(p):
        return copy(
            handed.at[pl.ds(pl.multiple_of(p * 32, 32), 32)],
            rbuf.at[p, 0],
            hand_rows.at[p],
            r_piece.at[0],
            0,
            p,
        )

    def hand_next(k, way):
        at = cbuf.at[0, pl.ds(pl.multiple_of(k * CHUNK, CHUNK), CHUNK)]
        return copy(at, at, hand_line.at[way, k], c_recv.at[k], 2 + way * (n - 4), 0)

    def middle():
        load_rest()
        arrive(lead.at[0], lead_recv.at[0])
        w0 = inverse[0]
        l10 = dot_nt(lead[0], w0)
        w10[...] = dot_nn(l10, w0)
        arrive(lead.at[1], lead_recv.at[1])
        work[...] = lead[1] - dot_nt(l10, l10)
        enter()
        signal(go_plane, 1, 0)
        hand(0).start()
        hand(1).start()

    @pl.when(corner)
    def _():
        work[...] = panel[0:NB, :]

        def block(b, carry):
            factor(work, solved_rows, upper.at[b], inverse.at[b])

            @pl.when(b == 0)
            def _():
                middle()

            return carry

        lax.fori_loop(0, 2, block, 0)
        wown[:, 0] = inverse[0].reshape(n, 8, NB)
        wown[:, 1] = -dot_nn(inverse[1], w10[...]).reshape(n, 8, NB)
        wown[:, 2] = inverse[1].reshape(n, 8, NB)
        span(0, n, lambda p: w_scatter(p).start())
        diagonal().start()
        rbuf[0, 0] = panel[0:32, :]
        plane_gather()
        pass_w()
        diag[...] = upper[0]

    @pl.when(no(corner))
    def _():
        enter()

        @pl.when(hub)
        def _():
            to_corner(0).start()

        @pl.when(last)
        def _():
            to_corner(1).start()

        @pl.when(r == 8)
        def _():
            signal(go_line, 1, c)

        @pl.when(z == 6)
        def _():
            signal(go_down, jnp.where(c == 0, 1, r - 12), c)

        @pl.when(both(r == 0, c == 1))
        def _():
            signal(go_plane, 1, 1)

        @pl.when(z == 0)
        def _():
            span(0, CHUNKS, line_up)

        load_rest()

        @pl.when(both(r == 1, left))
        def _():
            pl.semaphore_wait(go_plane, 1)

        @pl.when(left)
        def _():
            plane_scatter()

        @pl.when(hub)
        def _():
            arrive(handed, hand_recv.at[0])
            each(lambda p: hand_scatter(p).start())
            arrive(cbuf.at[0], hand_recv.at[1])
            span(0, CHUNKS, lambda k: hand_next(k, 0).start())
            pl.semaphore_wait(go_down, 2)
            span(0, CHUNKS, lambda k: hand_next(k, 1).start())

        @pl.when(z == 0)
        def _():
            @pl.when(no(hub))
            def _():
                pl.semaphore_wait(go_down, 1)

            span(0, CHUNKS, line_down)

        early = jnp.where(z == 1, CHUNKS // 2, jnp.where(z == 2, 1, 0))
        mid = jnp.where(z == 4, CHUNKS // 2, jnp.where(z == 5, 5, CHUNKS))

        @pl.when(z > 0)
        def _():
            span(0, early, line_relay)

        plane_gather()

        @pl.when(z > 0)
        def _():
            span(early, mid, line_relay)

        pass_w()

        @pl.when(z > 0)
        def _():
            span(mid, CHUNKS, line_relay)

    @pl.when(z == 0)
    def _():
        cbuf[core] = xv[0:512, :]

    def w_wait(k):
        p = other(c, k)
        arrive(wbuf.at[p], w_gather.at[p])

    def r_wait(k):
        p = other(c, k)
        arrive(rbuf.at[p], r_gather.at[p])

    def c_wait(k):
        arrive(cbuf.at[1 - core, pl.ds(pl.multiple_of(k * CHUNK, CHUNK), CHUNK)], c_pair.at[k])

    @pl.when(no(hub))
    def _():
        span(0, CHUNKS, c_wait)

    for h in range(2):
        for b in range(4):
            ac[h * NB : (h + 1) * NB, b * NB : (b + 1) * NB] = cbuf[h, pl.ds(b, NB, stride=4), :]
    each(r_wait)
    each(w_wait)
    w00 = wbuf[:, 0].reshape(NB, NB)
    w01 = wbuf[:, 1].reshape(NB, NB)
    w11 = wbuf[:, 2].reshape(NB, NB)
    r0 = rbuf[:, 0].reshape(4 * NB, NB)
    r1 = rbuf[:, 1].reshape(4 * NB, NB)
    rows = jnp.concatenate([r0, r1], axis=1)
    lower = jnp.concatenate(
        [
            jnp.concatenate([w00, jnp.zeros((NB, NB), F32)], axis=1),
            jnp.concatenate([w01, w11], axis=1),
        ],
        axis=0,
    )
    pr[...] = dot_nt(rows, lower)
    pc[...] = dot_nn(lower, ac[...])

    @pl.when(last)
    def _():
        arrive(diag, diag_recv)

    @pl.when(corner)
    def _():
        span(0, n, lambda p: w_scatter(p).wait_send())
        diagonal().wait_send()
        hand(0).wait_send()
        hand(1).wait_send()

    @pl.when(hub)
    def _():
        to_corner(0).wait_send()
        each(lambda p: hand_scatter(p).wait_send())
        span(0, CHUNKS, lambda k: hand_next(k, 0).wait_send())
        span(0, CHUNKS, lambda k: hand_next(k, 1).wait_send())

    @pl.when(last)
    def _():
        to_corner(1).wait_send()

    @pl.when(both(left, no(corner)))
    def _():
        each(lambda k: r_scatter(k).wait_send())

    @pl.when(r == 1)
    def _():
        each(lambda k: w_down(k).wait_send())

    @pl.when(either(both(z == 0, no(corner)), up))
    def _():
        span(0, CHUNKS, lambda k: c_next(k, 0, chunk(k)).wait_send())

    @pl.when(either(both(z == 0, no(corner)), down))
    def _():
        span(0, CHUNKS, lambda k: c_next(k, 1, chunk(k)).wait_send())

    @pl.when(no(corner))
    def _():
        span(0, CHUNKS, lambda k: c_beside(k, chunk(k)).wait_send())

    each(lambda k: r_across(k).wait_send())
    each(lambda k: w_across(k).wait_send())


def update_kernel(x, pr, pc, diag, out, parts, sems):
    r = lax.axis_index("row")
    c = lax.axis_index("col")
    both = jnp.logical_and

    def store(a):
        return pltpu.make_async_copy(parts.at[a], out.at[pl.ds(a * 512, 512)], sems.at[a])

    for a in range(4):
        at = slice(a * NB, (a + 1) * NB)

        def put(b, value):
            parts[a, pl.ds(b, NB, stride=4), :] = value

        def update():
            delta = dot_nn(pr[at, :], pc[...])
            for b in range(4):
                put(b, x[pl.ds(a * 512 + b, NB, stride=4), :] - delta[:, b * NB : (b + 1) * NB])

            @pl.when(c == 0)
            def _():
                put(0, pr[at, 0:NB])

            @pl.when(c == 1)
            def _():
                put(0, pr[at, NB:])

        if a > 0:
            update()
        else:

            @pl.when(r < 2)
            def _():
                parts[0] = jnp.zeros((512, NB), F32)

                @pl.when(both(r == 1, c == 0))
                def _():
                    put(0, pr[at, 0:NB])

                @pl.when(both(r == c, c < 2))
                def _():
                    put(0, diag[...].T)

            @pl.when(r >= 2)
            def _():
                update()

        store(a).start()

    for a in range(4):
        store(a).wait()


def per_device(matrix):
    n = lax.axis_size("row")
    flat = matrix.reshape(2048, NB)
    dma = pltpu.SemaphoreType.DMA
    square = pltpu.VMEM((NB, NB), F32)
    whole = pl.BlockSpec(memory_space=pltpu.VMEM)
    flat = pltpu.with_memory_space_constraint(flat, pltpu.HBM)
    pr, pc, diag, x = pl.pallas_call(
        functools.partial(gather_kernel, n),
        out_shape=[
            pltpu.VMEM((4 * NB, 2 * NB), F32),
            pltpu.VMEM((2 * NB, 4 * NB), F32),
            square,
            pltpu.VMEM((2048, NB), F32),
        ],
        in_specs=[pl.BlockSpec(memory_space=pl.ANY)],
        out_specs=[whole] * 4,
        scratch_shapes=[
            pltpu.VMEM((512, NB), F32),
            pltpu.VMEM((2, NB, NB), F32),
            pltpu.VMEM((n, 2, 32, NB), F32),
            pltpu.VMEM((2, 512, NB), F32),
            pltpu.VMEM((n, 3, 8, NB), F32),
            pltpu.VMEM((n, 3, 8, NB), F32),
            pltpu.VMEM((2 * NB, 4 * NB), F32),
            square,
            square,
            pltpu.VMEM((2, NB, NB), F32),
            pltpu.VMEM((2, NB, NB), F32),
            square,
            pltpu.VMEM((512, NB), F32),
            dma((2,)),
            dma((2,)),
            dma,
            dma,
            dma,
            pltpu.SemaphoreType.REGULAR,
            pltpu.SemaphoreType.REGULAR,
            pltpu.SemaphoreType.REGULAR,
            dma((2,)),
            dma((2,)),
            dma((n,)),
            dma((2, CHUNKS)),
            dma((2,)),
            dma((n,)),
            dma((n,)),
            dma((n,)),
            dma((CHUNKS,)),
            dma((2, CHUNKS)),
            dma((CHUNKS,)),
            dma((CHUNKS,)),
            dma,
            dma((n,)),
            dma((n,)),
            dma((n,)),
            dma((n,)),
        ],
        compiler_params=pltpu.CompilerParams(
            collective_id=0, has_side_effects=True, vmem_limit_bytes=24 * 1024 * 1024
        ),
    )(flat)
    out = pl.pallas_call(
        update_kernel,
        out_shape=pltpu.HBM((2048, NB), F32),
        in_specs=[whole] * 4,
        out_specs=pl.BlockSpec(memory_space=pltpu.HBM),
        scratch_shapes=[pltpu.VMEM((4, 512, NB), F32), dma((4,))],
        compiler_params=pltpu.CompilerParams(vmem_limit_bytes=24 * 1024 * 1024),
    )(x, pr, pc, diag)
    return out.reshape(matrix.shape)


def solution(mesh):
    specs = P(None, "row", None, None, "col", None)
    return jax.shard_map(
        per_device, mesh=mesh, in_specs=(specs,), out_specs=specs, check_vma=False
    )
```

profile of v0, /device:TPU:160, one launch (start us, length us, event | category | flops | bytes accessed | tf_op | source)
XLA Modules:
  0.0 31.2 jit_solution(9258403460698218894)
XLA Ops:
  0.0 28.8 %shard_map.17 = (f32[512,256]{1,0:T(8,128)S(1)}, f32[256,512]{1,0:T(8,128)S(1)}, f32[128,128]{1,0:T(8,128)S(1)}, f32[2048,128]{1,0:T(8,128)S(1)}) custom-call(f32[2048,128]{1,0:T(8,128)} %bitcast.4), custom_call_target="tpu_custom_call" | custom-call | tf_op jit(solution)/shard_map/pallas_call | solution.py:610
  28.8 2.5 %shard_map.18 = f32[2048,128]{1,0:T(8,128)} custom-call(f32[2048,128]{1,0:T(8,128)S(1)} %get-tuple-element.9.x, f32[512,256]{1,0:T(8,128)S(1)} %get-tuple-element.10.pr, f32[256,512]{1,0:T(8,128)S(1)} %get-tuple-element.11.pc, f32[128,128]{1,0:T(8,128)S(1)} %get-tuple-element.12.diag), custom_call_target="tpu_custom_call" | custom-call | tf_op jit(solution)/shard_map/pallas_call | solution.py:664
where the time goes:
time: 31.3 us; the launch traced here: 31.2 us
  Pallas kernels  31.2 us (100%)
    pallas_call x1, Pallas kernels, per_device(): pl.pallas_call(functools.partial(gather_kernel, n), out_shape=[pltpu.VMEM...  28.8 us
    pallas_call x1, Pallas kernels, per_device(): pl.pallas_call(update_kernel, out_shape=pltpu.HBM((2048, NB), F32), in_sp...  2.46 us

commit v1 on v0

--- a/solution.py
+++ b/solution.py
@@ -14,6 +14,8 @@
 LOOK = 2
 CHUNK = 64
 CHUNKS = 512 // CHUNK
+EARLY = (0, 6, 4, 2, 0, 0, 0, 1)
+MID = (0, 8, 8, 8, 6, 0, 2, 4)
 
 
 def dot_nn(a, b):
@@ -133,6 +135,8 @@
     w_send_a,
     w_send_b,
     w_send_c,
+    w_pair,
+    w_pair_send,
 ):
     r = lax.axis_index("row")
     c = lax.axis_index("col")
@@ -175,7 +179,8 @@
 
     hub = both(r == 1, c == 0)
     barrier = pltpu.get_barrier_semaphore()
-    before = jnp.where(z < 5, r - 2, jnp.where(z < 7, r + 2, r - 2))
+    door = jnp.where(left, 2, 12)
+    before = jnp.where(z < 5, r - 2, jnp.where(z < 7, r + 2, door + core))
     signal(barrier, pair, c)
 
     @pl.when(z > 0)
@@ -188,11 +193,11 @@
 
     @pl.when(either(hub, both(z == 0, c != 0)))
     def _():
-        signal(barrier, r + 12, c)
+        signal(barrier, door + core, c)
 
     @pl.when(hub)
     def _():
-        signal(barrier, 12, c)
+        signal(barrier, door, c)
 
     for k in range(2):
 
@@ -224,10 +229,11 @@
             panel[NB:, :] = xv[pl.ds(512, 384, stride=4), :]
 
     def enter():
-        after = jnp.where(either(z == 4, z == 5), 0, jnp.where(z == 6, 3, 1))
+        after = jnp.where(either(z == 4, z == 5), 0, 1)
         heard = (
             1
             + after
+            + jnp.where(z == door // 2, 2, 0)
             + jnp.where(r == 8, n - 2, 0)
             + jnp.where(both(z > 0, left), n - 1, 0)
             + jnp.where(both(r == 0, left), 2 * (n - 1), 0)
@@ -311,7 +317,7 @@
         return copy(wown.at[p], wbuf.at[p], w_send_a.at[p], w_piece, 1, p)
 
     def w_down(k):
-        p = other(r, k)
+        p = lax.rem(r + 2 * k, n)
         return w_copy(w_send_b.at[p], w_piece, p, c)
 
     def w_across(k):
@@ -321,13 +327,17 @@
     def diagonal():
         return copy(upper.at[1], diag, diag_send, diag_recv, 1, 1)
 
+    def w_beside(g):
+        part = wbuf.at[pl.ds(4 * g, 4)]
+        return copy(part, part, w_pair_send.at[g], w_pair.at[g], pair, c)
+
     def pass_w():
         arrive(wbuf.at[c], w_piece)
 
         @pl.when(r == 1)
         def _():
             pl.semaphore_wait(go_line, 1)
-            each(lambda k: w_down(k).start())
+            span(1, n // 2, lambda k: w_down(k).start())
 
         each(lambda k: w_across(k).start())
 
@@ -353,6 +363,8 @@
     def middle():
         load_rest()
         arrive(lead.at[0], lead_recv.at[0])
+        hand(0).start()
+        hand(1).start()
         w0 = inverse[0]
         l10 = dot_nt(lead[0], w0)
         w10[...] = dot_nn(l10, w0)
@@ -360,8 +372,99 @@
         work[...] = lead[1] - dot_nt(l10, l10)
         enter()
         signal(go_plane, 1, 0)
-        hand(0).start()
-        hand(1).start()
+
+    @pl.when(no(corner))
+    def _():
+        enter()
+
+        @pl.when(hub)
+        def _():
+            to_corner(0).start()
+
+        @pl.when(last)
+        def _():
+            to_corner(1).start()
+
+        @pl.when(r == 8)
+        def _():
+            signal(go_line, 1, c)
+
+        @pl.when(z == door // 2)
+        def _():
+            signal(go_down, jnp.where(c == 0, 1, core), c)
+
+        @pl.when(both(r == 0, c == 1))
+        def _():
+            signal(go_plane, 1, 1)
+
+        @pl.when(z == 0)
+        def _():
+            span(0, CHUNKS, line_up)
+
+        load_rest()
+
+        @pl.when(both(r == 1, left))
+        def _():
+            pl.semaphore_wait(go_plane, 1)
+
+        @pl.when(left)
+        def _():
+            plane_scatter()
+
+        @pl.when(hub)
+        def _():
+            arrive(handed, hand_recv.at[0])
+            each(lambda p: hand_scatter(p).start())
+            arrive(cbuf.at[0], hand_recv.at[1])
+            span(0, CHUNKS, lambda k: hand_next(k, 0).start())
+            pl.semaphore_wait(go_down, 2)
+            span(0, CHUNKS, lambda k: hand_next(k, 1).start())
+
+        @pl.when(z == 0)
+        def _():
+            @pl.when(no(hub))
+            def _():
+                pl.semaphore_wait(go_down, 1)
+
+            span(0, CHUNKS, line_down)
+
+        def by_plane(counts):
+            value = counts[0]
+            for k in range(1, 8):
+                value = jnp.where(z == k, counts[k], value)
+            return value
+
+        early = by_plane(EARLY)
+        mid = by_plane(MID)
+
+        @pl.when(z > 0)
+        def _():
+            span(0, early, line_relay)
+
+        plane_gather()
+
+        @pl.when(z > 0)
+        def _():
+            span(early, mid, line_relay)
+
+        @pl.when(core == 1)
+        def _():
+            pass_w()
+
+        @pl.when(z > 0)
+        def _():
+            span(mid, CHUNKS, line_relay)
+
+        @pl.when(core == 1)
+        def _():
+            for g in range(4):
+                for p in range(4 * g, 4 * g + 4):
+
+                    @pl.when(c != p)
+                    def _():
+                        arrive(wbuf.at[p], w_gather.at[p])
+
+                w_beside(g).start()
 
     @pl.when(corner)
     def _():
@@ -384,90 +487,11 @@
         diagonal().start()
         rbuf[0, 0] = panel[0:32, :]
         plane_gather()
-        pass_w()
         diag[...] = upper[0]
 
-    @pl.when(no(corner))
-    def _():
-        enter()
-
-        @pl.when(hub)
-        def _():
-            to_corner(0).start()
-
-        @pl.when(last)
-        def _():
-            to_corner(1).start()
-
-        @pl.when(r == 8)
-        def _():
-            signal(go_line, 1, c)
-
-        @pl.when(z == 6)
-        def _():
-            signal(go_down, jnp.where(c == 0, 1, r - 12), c)
-
-        @pl.when(both(r == 0, c == 1))
-        def _():
-            signal(go_plane, 1, 1)
-
-        @pl.when(z == 0)
-        def _():
-            span(0, CHUNKS, line_up)
-
-        load_rest()
-
-        @pl.when(both(r == 1, left))
-        def _():
-            pl.semaphore_wait(go_plane, 1)
-
-        @pl.when(left)
-        def _():
-            plane_scatter()
-
-        @pl.when(hub)
-        def _():
-            arrive(handed, hand_recv.at[0])
-            each(lambda p: hand_scatter(p).start())
-            arrive(cbuf.at[0], hand_recv.at[1])
-            span(0, CHUNKS, lambda k: hand_next(k, 0).start())
-            pl.semaphore_wait(go_down, 2)
-            span(0, CHUNKS, lambda k: hand_next(k, 1).start())
-
-        @pl.when(z == 0)
-        def _():
-            @pl.when(no(hub))
-            def _():
-                pl.semaphore_wait(go_down, 1)
-
-            span(0, CHUNKS, line_down)
-
-        early = jnp.where(z == 1, CHUNKS // 2, jnp.where(z == 2, 1, 0))
-        mid = jnp.where(z == 4, CHUNKS // 2, jnp.where(z == 5, 5, CHUNKS))
-
-        @pl.when(z > 0)
-        def _():
-            span(0, early, line_relay)
-
-        plane_gather()
-
-        @pl.when(z > 0)
-        def _():
-            span(early, mid, line_relay)
-
-        pass_w()
-
-        @pl.when(z > 0)
-        def _():
-            span(mid, CHUNKS, line_relay)
-
     @pl.when(z == 0)
     def _():
         cbuf[core] = xv[0:512, :]
-
-    def w_wait(k):
-        p = other(c, k)
-        arrive(wbuf.at[p], w_gather.at[p])
 
     def r_wait(k):
         p = other(c, k)
@@ -484,7 +508,12 @@
         for b in range(4):
             ac[h * NB : (h + 1) * NB, b * NB : (b + 1) * NB] = cbuf[h, pl.ds(b, NB, stride=4), :]
     each(r_wait)
-    each(w_wait)
+
+    @pl.when(core == 0)
+    def _():
+        for g in range(4):
+            arrive(wbuf.at[pl.ds(4 * g, 4)], w_pair.at[g])
+
     w00 = wbuf[:, 0].reshape(NB, NB)
     w01 = wbuf[:, 1].reshape(NB, NB)
     w11 = wbuf[:, 2].reshape(NB, NB)
@@ -529,7 +558,7 @@
 
     @pl.when(r == 1)
     def _():
-        each(lambda k: w_down(k).wait_send())
+        span(1, n // 2, lambda k: w_down(k).wait_send())
 
     @pl.when(either(both(z == 0, no(corner)), up))
     def _():
@@ -544,7 +573,12 @@
         span(0, CHUNKS, lambda k: c_beside(k, chunk(k)).wait_send())
 
     each(lambda k: r_across(k).wait_send())
-    each(lambda k: w_across(k).wait_send())
+
+    @pl.when(core == 1)
+    def _():
+        each(lambda k: w_across(k).wait_send())
+        for g in range(4):
+            w_beside(g).wait_send()
 
 
 def update_kernel(x, pr, pc, diag, out, parts, sems):
@@ -656,6 +690,8 @@
             dma((n,)),
             dma((n,)),
             dma((n,)),
+            dma((4,)),
+            dma((4,)),
         ],
         compiler_params=pltpu.CompilerParams(
             collective_id=0, has_side_effects=True, vmem_limit_bytes=24 * 1024 * 1024

time: 31.3 us -> 29.3 us (0.936)
  the two profiles are of different devices: /device:TPU:160 before, /device:TPU:32 now
where the time goes in v1:
time: 29.3 us; the launch traced here: 29.2 us
  Pallas kernels  29.2 us (100%)
    pallas_call x1, Pallas kernels, per_device(): pl.pallas_call(functools.partial(gather_kernel, n), out_shape=[pltpu.VMEM...  26.8 us
    pallas_call x1, Pallas kernels, per_device(): pl.pallas_call(update_kernel, out_shape=pltpu.HBM((2048, NB), F32), in_sp...  2.46 us

profile of v1, /device:TPU:32, one launch (start us, length us, event | category | flops | bytes accessed | tf_op | source)
XLA Modules:
  0.0 29.2 jit_solution(2414857285307914822)
XLA Ops:
  0.0 26.8 %shard_map.17 = (f32[512,256]{1,0:T(8,128)S(1)}, f32[256,512]{1,0:T(8,128)S(1)}, f32[128,128]{1,0:T(8,128)S(1)}, f32[2048,128]{1,0:T(8,128)S(1)}) custom-call(f32[2048,128]{1,0:T(8,128)} %bitcast.4), custom_call_target="tpu_custom_call" | custom-call | tf_op jit(solution)/shard_map/pallas_call | solution.py:644
  26.8 2.5 %shard_map.18 = f32[2048,128]{1,0:T(8,128)} custom-call(f32[2048,128]{1,0:T(8,128)S(1)} %get-tuple-element.9.x, f32[512,256]{1,0:T(8,128)S(1)} %get-tuple-element.10.pr, f32[256,512]{1,0:T(8,128)S(1)} %get-tuple-element.11.pc, f32[128,128]{1,0:T(8,128)S(1)} %get-tuple-element.12.diag), custom_call_target="tpu_custom_call" | custom-call | tf_op jit(solution)/shard_map/pallas_call | solution.py:700

commit v2 on v1

--- a/solution.py
+++ b/solution.py
@@ -263,6 +263,17 @@
         each(lambda k: r_scatter(k).start())
         rbuf[c, c] = panel[pl.ds(pl.multiple_of(c * 32, 32), 32), :]
 
+    def r_batch(first):
+        def send(k):
+            p = other(c, k)
+            early = either(p < 4, p >= 12)
+
+            @pl.when(early if first else no(early))
+            def _():
+                r_across(k).start()
+
+        each(send)
+
     def plane_gather():
         @pl.when(c != 0)
         def _():
@@ -272,7 +283,11 @@
         def _():
             arrive(rbuf.at[c, 1], r_piece.at[1])
 
-        each(lambda k: r_across(k).start())
+        r_batch(True)
+
+        @pl.when(core == 0)
+        def _():
+            r_batch(False)
 
     def chunk(k):
         return cbuf.at[core, pl.ds(pl.multiple_of(k * CHUNK, CHUNK), CHUNK)]
@@ -339,7 +354,16 @@
             pl.semaphore_wait(go_line, 1)
             span(1, n // 2, lambda k: w_down(k).start())
 
-        each(lambda k: w_across(k).start())
+        for near in (True, False):
+
+            def send(k):
+                @pl.when((other(c, k) < 4) == near)
+                def _():
+                    w_across(k).start()
+
+            each(send)
+
+        r_batch(False)
 
     def hand(b):
         src = panel if b == 0 else xv.at[pl.ds(0, 512)]
@@ -483,7 +507,8 @@
         wown[:, 0] = inverse[0].reshape(n, 8, NB)
         wown[:, 1] = -dot_nn(inverse[1], w10[...]).reshape(n, 8, NB)
         wown[:, 2] = inverse[1].reshape(n, 8, NB)
-        span(0, n, lambda p: w_scatter(p).start())
+        for p in range(n):
+            w_scatter((p + n // 2) % n).start()
         diagonal().start()
         rbuf[0, 0] = panel[0:32, :]
         plane_gather()

time: 29.3 us -> 28.2 us (0.962)
  the two profiles are of different devices: /device:TPU:32 before, /device:TPU:37 now
where the time goes in v2:
time: 28.2 us; the launch traced here: 28.1 us
  Pallas kernels  28.1 us (100%)
    pallas_call x1, Pallas kernels, per_device(): pl.pallas_call(functools.partial(gather_kernel, n), out_shape=[pltpu.VMEM...  25.6 us
    pallas_call x1, Pallas kernels, per_device(): pl.pallas_call(update_kernel, out_shape=pltpu.HBM((2048, NB), F32), in_sp...  2.45 us

profile of v2, /device:TPU:37, one launch (start us, length us, event | category | flops | bytes accessed | tf_op | source)
XLA Modules:
  0.0 28.1 jit_solution(5955976282196368739)
XLA Ops:
  0.0 25.6 %shard_map.17 = (f32[512,256]{1,0:T(8,128)S(1)}, f32[256,512]{1,0:T(8,128)S(1)}, f32[128,128]{1,0:T(8,128)S(1)}, f32[2048,128]{1,0:T(8,128)S(1)}) custom-call(f32[2048,128]{1,0:T(8,128)} %bitcast.4), custom_call_target="tpu_custom_call" | custom-call | tf_op jit(solution)/shard_map/pallas_call | solution.py:669
  25.6 2.5 %shard_map.18 = f32[2048,128]{1,0:T(8,128)} custom-call(f32[2048,128]{1,0:T(8,128)S(1)} %get-tuple-element.9.x, f32[512,256]{1,0:T(8,128)S(1)} %get-tuple-element.10.pr, f32[256,512]{1,0:T(8,128)S(1)} %get-tuple-element.11.pc, f32[128,128]{1,0:T(8,128)S(1)} %get-tuple-element.12.diag), custom_call_target="tpu_custom_call" | custom-call | tf_op jit(solution)/shard_map/pallas_call | solution.py:725

commit v3 on v2

--- a/solution.py
+++ b/solution.py
@@ -141,6 +141,7 @@
     r = lax.axis_index("row")
     c = lax.axis_index("col")
     z = r // 2
+    x = c // 4
     core = lax.rem(r, 2)
     pair = r + 1 - 2 * core
     both, either, no = jnp.logical_and, jnp.logical_or, jnp.logical_not
@@ -249,7 +250,7 @@
         return copy(
             panel.at[pl.ds(pl.multiple_of(p * 32, 32), 32)],
             rbuf.at[p, c],
-            r_send_a.at[p],
+            r_send_a,
             r_piece.at[c],
             r,
             p,
@@ -257,10 +258,10 @@
 
     def r_across(k):
         p = other(c, k)
-        return copy(rbuf.at[c], rbuf.at[c], r_send_b.at[p], r_gather.at[c], r, p)
+        return copy(rbuf.at[c], rbuf.at[c], r_send_b, r_gather, r, p)
 
     def plane_scatter():
-        each(lambda k: r_scatter(k).start())
+        each(lambda k: r_scatter(lax.rem(k + n // 2 - 2, n - 1) + 1).start())
         rbuf[c, c] = panel[pl.ds(pl.multiple_of(c * 32, 32), 32), :]
 
     def r_batch(first):
@@ -297,10 +298,10 @@
 
     def c_next(k, way, src):
         there = lax.rem(r + 2 + way * (n - 4), n)
-        return copy(src, chunk(k), c_send.at[way, k], c_recv.at[k], there, c)
+        return copy(src, chunk(k), c_send.at[way], c_recv.at[k], there, c)
 
     def c_beside(k, src):
-        return copy(src, chunk(k), c_pair_send.at[k], c_pair.at[k], pair, c)
+        return copy(src, chunk(k), c_pair_send, c_pair, pair, c)
 
     def line_up(k):
         c_next(k, 0, first_chunk(k)).start()
@@ -329,22 +330,22 @@
         return copy(wbuf.at[c], wbuf.at[c], send, recv, row, col)
 
     def w_scatter(p):
-        return copy(wown.at[p], wbuf.at[p], w_send_a.at[p], w_piece, 1, p)
+        return copy(wown.at[p], wbuf.at[p], w_send_a, w_piece, 1, p)
 
     def w_down(k):
         p = lax.rem(r + 2 * k, n)
-        return w_copy(w_send_b.at[p], w_piece, p, c)
+        return w_copy(w_send_b, w_piece, p, c)
 
     def w_across(k):
         p = other(c, k)
-        return w_copy(w_send_c.at[p], w_gather.at[c], r, p)
+        return w_copy(w_send_c, w_gather.at[c // 4], r, p)
 
     def diagonal():
         return copy(upper.at[1], diag, diag_send, diag_recv, 1, 1)
 
     def w_beside(g):
         part = wbuf.at[pl.ds(4 * g, 4)]
-        return copy(part, part, w_pair_send.at[g], w_pair.at[g], pair, c)
+        return copy(part, part, w_pair_send, w_pair, pair, c)
 
     def pass_w():
         arrive(wbuf.at[c], w_piece)
@@ -374,7 +375,7 @@
         return copy(
             handed.at[pl.ds(pl.multiple_of(p * 32, 32), 32)],
             rbuf.at[p, 0],
-            hand_rows.at[p],
+            hand_rows,
             r_piece.at[0],
             0,
             p,
@@ -382,7 +383,7 @@
 
     def hand_next(k, way):
         at = cbuf.at[0, pl.ds(pl.multiple_of(k * CHUNK, CHUNK), CHUNK)]
-        return copy(at, at, hand_line.at[way, k], c_recv.at[k], 2 + way * (n - 4), 0)
+        return copy(at, at, hand_line.at[way], c_recv.at[k], 2 + way * (n - 4), 0)
 
     def middle():
         load_rest()
@@ -482,11 +483,13 @@
         @pl.when(core == 1)
         def _():
             for g in range(4):
-                for p in range(4 * g, 4 * g + 4):
-
-                    @pl.when(c != p)
-                    def _():
-                        arrive(wbuf.at[p], w_gather.at[p])
+                @pl.when(x == g)
+                def _():
+                    arrive(wbuf.at[pl.ds(4 * g, 3)], w_gather.at[g])
+
+                @pl.when(x != g)
+                def _():
+                    arrive(wbuf.at[pl.ds(4 * g, 4)], w_gather.at[g])
 
                 w_beside(g).start()
 
@@ -518,33 +521,21 @@
     def _():
         cbuf[core] = xv[0:512, :]
 
-    def r_wait(k):
-        p = other(c, k)
-        arrive(rbuf.at[p], r_gather.at[p])
-
-    def c_wait(k):
-        arrive(cbuf.at[1 - core, pl.ds(pl.multiple_of(k * CHUNK, CHUNK), CHUNK)], c_pair.at[k])
-
     @pl.when(no(hub))
     def _():
-        span(0, CHUNKS, c_wait)
+        arrive(cbuf.at[1 - core], c_pair)
 
     for h in range(2):
         for b in range(4):
             ac[h * NB : (h + 1) * NB, b * NB : (b + 1) * NB] = cbuf[h, pl.ds(b, NB, stride=4), :]
-    each(r_wait)
 
     @pl.when(core == 0)
     def _():
-        for g in range(4):
-            arrive(wbuf.at[pl.ds(4 * g, 4)], w_pair.at[g])
+        arrive(wbuf, w_pair)
 
     w00 = wbuf[:, 0].reshape(NB, NB)
     w01 = wbuf[:, 1].reshape(NB, NB)
     w11 = wbuf[:, 2].reshape(NB, NB)
-    r0 = rbuf[:, 0].reshape(4 * NB, NB)
-    r1 = rbuf[:, 1].reshape(4 * NB, NB)
-    rows = jnp.concatenate([r0, r1], axis=1)
     lower = jnp.concatenate(
         [
             jnp.concatenate([w00, jnp.zeros((NB, NB), F32)], axis=1),
@@ -552,16 +543,21 @@
         ],
         axis=0,
     )
-    pr[...] = dot_nt(rows, lower)
     pc[...] = dot_nn(lower, ac[...])
+    arrive(rbuf.at[pl.ds(0, n - 1)], r_gather)
+    r0 = rbuf[:, 0].reshape(4 * NB, NB)
+    r1 = rbuf[:, 1].reshape(4 * NB, NB)
+    pr[...] = dot_nt(jnp.concatenate([r0, r1], axis=1), lower)
 
     @pl.when(last)
     def _():
         arrive(diag, diag_recv)
 
+    most = n - 1
+
     @pl.when(corner)
     def _():
-        span(0, n, lambda p: w_scatter(p).wait_send())
+        arrive(wown, w_send_a)
         diagonal().wait_send()
         hand(0).wait_send()
         hand(1).wait_send()
@@ -569,9 +565,9 @@
     @pl.when(hub)
     def _():
         to_corner(0).wait_send()
-        each(lambda p: hand_scatter(p).wait_send())
-        span(0, CHUNKS, lambda k: hand_next(k, 0).wait_send())
-        span(0, CHUNKS, lambda k: hand_next(k, 1).wait_send())
+        arrive(handed.at[pl.ds(0, 32 * most)], hand_rows)
+        arrive(cbuf.at[0], hand_line.at[0])
+        arrive(cbuf.at[0], hand_line.at[1])
 
     @pl.when(last)
     def _():
@@ -579,31 +575,30 @@
 
     @pl.when(both(left, no(corner)))
     def _():
-        each(lambda k: r_scatter(k).wait_send())
+        arrive(panel.at[pl.ds(0, 32 * most)], r_send_a)
 
     @pl.when(r == 1)
     def _():
-        span(1, n // 2, lambda k: w_down(k).wait_send())
+        arrive(wbuf.at[pl.ds(0, n // 2 - 1)], w_send_b)
 
     @pl.when(either(both(z == 0, no(corner)), up))
     def _():
-        span(0, CHUNKS, lambda k: c_next(k, 0, chunk(k)).wait_send())
+        arrive(cbuf.at[core], c_send.at[0])
 
     @pl.when(either(both(z == 0, no(corner)), down))
     def _():
-        span(0, CHUNKS, lambda k: c_next(k, 1, chunk(k)).wait_send())
+        arrive(cbuf.at[core], c_send.at[1])
 
     @pl.when(no(corner))
     def _():
-        span(0, CHUNKS, lambda k: c_beside(k, chunk(k)).wait_send())
-
-    each(lambda k: r_across(k).wait_send())
+        arrive(cbuf.at[core], c_pair_send)
+
+    arrive(rbuf.at[pl.ds(0, most)], r_send_b)
 
     @pl.when(core == 1)
     def _():
-        each(lambda k: w_across(k).wait_send())
-        for g in range(4):
-            w_beside(g).wait_send()
+        arrive(wbuf.at[pl.ds(0, most)], w_send_c)
+        arrive(wbuf, w_pair_send)
 
 
 def update_kernel(x, pr, pc, diag, out, parts, sems):
@@ -700,23 +695,23 @@
             pltpu.SemaphoreType.REGULAR,
             dma((2,)),
             dma((2,)),
-            dma((n,)),
-            dma((2, CHUNKS)),
+            dma,
             dma((2,)),
-            dma((n,)),
-            dma((n,)),
-            dma((n,)),
+            dma((2,)),
+            dma,
+            dma,
+            dma,
             dma((CHUNKS,)),
-            dma((2, CHUNKS)),
-            dma((CHUNKS,)),
-            dma((CHUNKS,)),
-            dma,
-            dma((n,)),
-            dma((n,)),
-            dma((n,)),
-            dma((n,)),
+            dma((2,)),
+            dma,
+            dma,
+            dma,
             dma((4,)),
-            dma((4,)),
+            dma,
+            dma,
+            dma,
+            dma,
+            dma,
         ],
         compiler_params=pltpu.CompilerParams(
             collective_id=0, has_side_effects=True, vmem_limit_bytes=24 * 1024 * 1024

time: 28.2 us -> 26 us (0.922)
  Pallas kernels: 28.1 us -> 25.9 us
    pallas_call x1, Pallas kernels: 25.6 us -> 23.5 us  [per_device(): pl.pallas_call(functools.partial(gather_kernel, n), out_shape=[pltpu.VMEM...]
where the time goes in v3:
time: 26 us; the launch traced here: 25.9 us
  Pallas kernels  25.9 us (100%)
    pallas_call x1, Pallas kernels, per_device(): pl.pallas_call(functools.partial(gather_kernel, n), out_shape=[pltpu.VMEM...  23.5 us
    pallas_call x1, Pallas kernels, per_device(): pl.pallas_call(update_kernel, out_shape=pltpu.HBM((2048, NB), F32), in_sp...  2.45 us

profile of v3, /device:TPU:37, one launch (start us, length us, event | category | flops | bytes accessed | tf_op | source)
XLA Modules:
  0.0 25.9 jit_solution(2450498656117451)
XLA Ops:
  0.0 23.5 %shard_map.17 = (f32[512,256]{1,0:T(8,128)S(1)}, f32[256,512]{1,0:T(8,128)S(1)}, f32[128,128]{1,0:T(8,128)S(1)}, f32[2048,128]{1,0:T(8,128)S(1)}) custom-call(f32[2048,128]{1,0:T(8,128)} %bitcast.4), custom_call_target="tpu_custom_call" | custom-call | tf_op jit(solution)/shard_map/pallas_call | solution.py:664
  23.5 2.5 %shard_map.18 = f32[2048,128]{1,0:T(8,128)} custom-call(f32[2048,128]{1,0:T(8,128)S(1)} %get-tuple-element.9.x, f32[512,256]{1,0:T(8,128)S(1)} %get-tuple-element.10.pr, f32[256,512]{1,0:T(8,128)S(1)} %get-tuple-element.11.pc, f32[128,128]{1,0:T(8,128)S(1)} %get-tuple-element.12.diag), custom_call_target="tpu_custom_call" | custom-call | tf_op jit(solution)/shard_map/pallas_call | solution.py:720

commit v4 on v3

--- a/solution.py
+++ b/solution.py
@@ -12,10 +12,14 @@
 HIGHEST = lax.Precision.HIGHEST
 NB = 128
 LOOK = 2
+STARTS = (0, 128, 384, 512)
 CHUNK = 64
 CHUNKS = 512 // CHUNK
 EARLY = (0, 6, 4, 2, 0, 0, 0, 1)
 MID = (0, 8, 8, 8, 6, 0, 2, 4)
+R_FIRST = (0, 3)
+R_LATER = (1, 2)
+W_ORDER = (0, 1, 2, 3)
 
 
 def dot_nn(a, b):
@@ -142,6 +146,8 @@
     c = lax.axis_index("col")
     z = r // 2
     x = c // 4
+    y = lax.rem(c, 4)
+    ys = [lax.rem(y + j, 4) for j in range(4)]
     core = lax.rem(r, 2)
     pair = r + 1 - 2 * core
     both, either, no = jnp.logical_and, jnp.logical_or, jnp.logical_not
@@ -178,44 +184,45 @@
     def arrive(buffer, sem):
         pltpu.make_async_copy(buffer, buffer, sem).wait()
 
-    hub = both(r == 1, c == 0)
-    barrier = pltpu.get_barrier_semaphore()
-    door = jnp.where(left, 2, 12)
-    before = jnp.where(z < 5, r - 2, jnp.where(z < 7, r + 2, door + core))
-    signal(barrier, pair, c)
-
-    @pl.when(z > 0)
-    def _():
-        signal(barrier, before, c)
-
-    @pl.when(z != 4)
-    def _():
-        signal(barrier, 8, c)
-
-    @pl.when(either(hub, both(z == 0, c != 0)))
-    def _():
-        signal(barrier, door + core, c)
-
-    @pl.when(hub)
-    def _():
-        signal(barrier, door, c)
-
-    for k in range(2):
-
-        @pl.when(c != k)
-        def _():
-            signal(barrier, jnp.where(z > 0, r, 0), k)
-
-    @pl.when(corner)
-    def _():
-        signal(barrier, 1, 1)
-
     top = pltpu.make_async_copy(x_hbm.at[pl.ds(0, 512)], xv.at[pl.ds(0, 512)], load_sem.at[0])
     below = pltpu.make_async_copy(
         x_hbm.at[pl.ds(512, 1536)], xv.at[pl.ds(512, 1536)], load_sem.at[1]
     )
     top.start()
     below.start()
+
+    hub = both(r == 1, c == 0)
+    barrier = pltpu.get_barrier_semaphore()
+    door = jnp.where(left, 2, 12)
+    before = jnp.where(z < 5, r - 2, jnp.where(z < 7, r + 2, door + core))
+    signal(barrier, pair, c)
+
+    @pl.when(z > 0)
+    def _():
+        signal(barrier, before, c)
+
+    @pl.when(z != 4)
+    def _():
+        signal(barrier, 8, c)
+
+    @pl.when(either(hub, both(z == 0, c != 0)))
+    def _():
+        signal(barrier, door + core, c)
+
+    @pl.when(hub)
+    def _():
+        signal(barrier, door, c)
+
+    for k in range(2):
+
+        @pl.when(c != k)
+        def _():
+            signal(barrier, jnp.where(z > 0, r, 0), k)
+
+    @pl.when(corner)
+    def _():
+        signal(barrier, 1, 1)
+
     top.wait()
 
     @pl.when(left)
@@ -245,10 +252,9 @@
     def to_corner(b):
         return copy(panel.at[pl.ds(0, NB)], lead.at[b], lead_send, lead_recv.at[b], 0, 0)
 
-    def r_scatter(k):
-        p = other(c, k)
+    def r_scatter(p):
         return copy(
-            panel.at[pl.ds(pl.multiple_of(p * 32, 32), 32)],
+            panel.at[pl.ds(p * 32, 32)],
             rbuf.at[p, c],
             r_send_a,
             r_piece.at[c],
@@ -256,13 +262,28 @@
             p,
         )
 
-    def r_across(k):
-        p = other(c, k)
+    def r_across(p):
         return copy(rbuf.at[c], rbuf.at[c], r_send_b, r_gather, r, p)
 
     def plane_scatter():
-        each(lambda k: r_scatter(lax.rem(k + n // 2 - 2, n - 1) + 1).start())
+        for p in (*range(n // 2, n), *range(2, n // 2)):
+            r_scatter(p).start()
+        for p in range(2):
+
+            @pl.when(c != p)
+            def _():
+                r_scatter(p).start()
+
         rbuf[c, c] = panel[pl.ds(pl.multiple_of(c * 32, 32), 32), :]
+
+    def columns(make, xs):
+        for there in xs:
+            for j in (2, 1, 3, 0):
+                p = 4 * there + ys[j]
+
+                @pl.when(p != c)
+                def _():
+                    make(p).start()
 
     def r_batch(first):
         def send(k):
@@ -271,7 +292,7 @@
 
             @pl.when(early if first else no(early))
             def _():
-                r_across(k).start()
+                r_across(p).start()
 
         each(send)
 
@@ -336,8 +357,7 @@
         p = lax.rem(r + 2 * k, n)
         return w_copy(w_send_b, w_piece, p, c)
 
-    def w_across(k):
-        p = other(c, k)
+    def w_across(p):
         return w_copy(w_send_c, w_gather.at[c // 4], r, p)
 
     def diagonal():
@@ -353,17 +373,10 @@
         @pl.when(r == 1)
         def _():
             pl.semaphore_wait(go_line, 1)
-            span(1, n // 2, lambda k: w_down(k).start())
-
-        for near in (True, False):
-
-            def send(k):
-                @pl.when((other(c, k) < 4) == near)
-                def _():
-                    w_across(k).start()
-
-            each(send)
-
+            for k in range(1, n // 2):
+                w_down(k).start()
+
+        columns(w_across, W_ORDER)
         r_batch(False)
 
     def hand(b):
@@ -373,7 +386,7 @@
 
     def hand_scatter(p):
         return copy(
-            handed.at[pl.ds(pl.multiple_of(p * 32, 32), 32)],
+            handed.at[pl.ds(p * 32, 32)],
             rbuf.at[p, 0],
             hand_rows,
             r_piece.at[0],
@@ -439,7 +452,8 @@
         @pl.when(hub)
         def _():
             arrive(handed, hand_recv.at[0])
-            each(lambda p: hand_scatter(p).start())
+            for p in (*range(n // 2, n), *range(1, n // 2)):
+                hand_scatter(p).start()
             arrive(cbuf.at[0], hand_recv.at[1])
             span(0, CHUNKS, lambda k: hand_next(k, 0).start())
             pl.semaphore_wait(go_down, 2)
@@ -528,6 +542,39 @@
     for h in range(2):
         for b in range(4):
             ac[h * NB : (h + 1) * NB, b * NB : (b + 1) * NB] = cbuf[h, pl.ds(b, NB, stride=4), :]
+
+    most = n - 1
+
+    @pl.when(hub)
+    def _():
+        to_corner(0).wait_send()
+        arrive(handed.at[pl.ds(0, 32 * most)], hand_rows)
+        arrive(cbuf.at[0], hand_line.at[0])
+        arrive(cbuf.at[0], hand_line.at[1])
+
+    @pl.when(last)
+    def _():
+        to_corner(1).wait_send()
+
+    @pl.when(both(left, no(corner)))
+    def _():
+        arrive(panel.at[pl.ds(0, 32 * most)], r_send_a)
+
+    @pl.when(r == 1)
+    def _():
+        arrive(wbuf.at[pl.ds(0, n // 2 - 1)], w_send_b)
+
+    @pl.when(either(both(z == 0, no(corner)), up))
+    def _():
+        arrive(cbuf.at[core], c_send.at[0])
+
+    @pl.when(either(both(z == 0, no(corner)), down))
+    def _():
+        arrive(cbuf.at[core], c_send.at[1])
+
+    @pl.when(no(corner))
+    def _():
+        arrive(cbuf.at[core], c_pair_send)
 
     @pl.when(core == 0)
     def _():
@@ -553,8 +600,6 @@
     def _():
         arrive(diag, diag_recv)
 
-    most = n - 1
-
     @pl.when(corner)
     def _():
         arrive(wown, w_send_a)
@@ -562,37 +607,6 @@
         hand(0).wait_send()
         hand(1).wait_send()
 
-    @pl.when(hub)
-    def _():
-        to_corner(0).wait_send()
-        arrive(handed.at[pl.ds(0, 32 * most)], hand_rows)
-        arrive(cbuf.at[0], hand_line.at[0])
-        arrive(cbuf.at[0], hand_line.at[1])
-
-    @pl.when(last)
-    def _():
-        to_corner(1).wait_send()
-
-    @pl.when(both(left, no(corner)))
-    def _():
-        arrive(panel.at[pl.ds(0, 32 * most)], r_send_a)
-
-    @pl.when(r == 1)
-    def _():
-        arrive(wbuf.at[pl.ds(0, n // 2 - 1)], w_send_b)
-
-    @pl.when(either(both(z == 0, no(corner)), up))
-    def _():
-        arrive(cbuf.at[core], c_send.at[0])
-
-    @pl.when(either(both(z == 0, no(corner)), down))
-    def _():
-        arrive(cbuf.at[core], c_send.at[1])
-
-    @pl.when(no(corner))
-    def _():
-        arrive(cbuf.at[core], c_pair_send)
-
     arrive(rbuf.at[pl.ds(0, most)], r_send_b)
 
     @pl.when(core == 1)
@@ -607,18 +621,23 @@
     both = jnp.logical_and
 
     def store(a):
-        return pltpu.make_async_copy(parts.at[a], out.at[pl.ds(a * 512, 512)], sems.at[a])
-
-    for a in range(4):
-        at = slice(a * NB, (a + 1) * NB)
+        whole = pl.ds(4 * STARTS[a], 4 * (STARTS[a + 1] - STARTS[a]))
+        return pltpu.make_async_copy(parts.at[whole], out.at[whole], sems.at[a])
+
+    for a in range(len(STARTS) - 1):
+        at = slice(STARTS[a], STARTS[a + 1])
+        count = STARTS[a + 1] - STARTS[a]
+
+        def rows(b):
+            return pl.ds(4 * STARTS[a] + b, count, stride=4)
 
         def put(b, value):
-            parts[a, pl.ds(b, NB, stride=4), :] = value
+            parts[rows(b), :] = value
 
         def update():
             delta = dot_nn(pr[at, :], pc[...])
             for b in range(4):
-                put(b, x[pl.ds(a * 512 + b, NB, stride=4), :] - delta[:, b * NB : (b + 1) * NB])
+                put(b, x[rows(b), :] - delta[:, b * NB : (b + 1) * NB])
 
             @pl.when(c == 0)
             def _():
@@ -634,7 +653,7 @@
 
             @pl.when(r < 2)
             def _():
-                parts[0] = jnp.zeros((512, NB), F32)
+                parts[0:512, :] = jnp.zeros((512, NB), F32)
 
                 @pl.when(both(r == 1, c == 0))
                 def _():
@@ -650,7 +669,7 @@
 
         store(a).start()
 
-    for a in range(4):
+    for a in range(len(STARTS) - 1):
         store(a).wait()
 
 
@@ -722,7 +741,7 @@
         out_shape=pltpu.HBM((2048, NB), F32),
         in_specs=[whole] * 4,
         out_specs=pl.BlockSpec(memory_space=pltpu.HBM),
-        scratch_shapes=[pltpu.VMEM((4, 512, NB), F32), dma((4,))],
+        scratch_shapes=[pltpu.VMEM((2048, NB), F32), dma((len(STARTS) - 1,))],
         compiler_params=pltpu.CompilerParams(vmem_limit_bytes=24 * 1024 * 1024),
     )(x, pr, pc, diag)
     return out.reshape(matrix.shape)

time: 26 us -> 25.8 us (level); the launches traced: 25.9 us -> 25.4 us
  Pallas kernels: 25.9 us -> 25.4 us
where the time goes in v4:
time: 25.8 us; the launch traced here: 25.4 us
  Pallas kernels  25.4 us (98%)
    pallas_call x1, Pallas kernels, per_device(): pl.pallas_call(functools.partial(gather_kernel, n), out_shape=[pltpu.VMEM...  23.2 us
    pallas_call x1, Pallas kernels, per_device(): pl.pallas_call(update_kernel, out_shape=pltpu.HBM((2048, NB), F32), in_sp...  2.21 us

profile of v4, /device:TPU:37, one launch (start us, length us, event | category | flops | bytes accessed | tf_op | source)
XLA Modules:
  0.0 25.4 jit_solution(3678715718762878609)
XLA Ops:
  0.0 23.2 %shard_map.17 = (f32[512,256]{1,0:T(8,128)S(1)}, f32[256,512]{1,0:T(8,128)S(1)}, f32[128,128]{1,0:T(8,128)S(1)}, f32[2048,128]{1,0:T(8,128)S(1)}) custom-call(f32[2048,128]{1,0:T(8,128)} %bitcast.4), custom_call_target="tpu_custom_call" | custom-call | tf_op jit(solution)/shard_map/pallas_call | solution.py:683
  23.2 2.2 %shard_map.18 = f32[2048,128]{1,0:T(8,128)} custom-call(f32[2048,128]{1,0:T(8,128)S(1)} %get-tuple-element.9.x, f32[512,256]{1,0:T(8,128)S(1)} %get-tuple-element.10.pr, f32[256,512]{1,0:T(8,128)S(1)} %get-tuple-element.11.pc, f32[128,128]{1,0:T(8,128)S(1)} %get-tuple-element.12.diag), custom_call_target="tpu_custom_call" | custom-call | tf_op jit(solution)/shard_map/pallas_call | solution.py:739

commit v5 on v4

--- a/solution.py
+++ b/solution.py
@@ -12,7 +12,7 @@
 HIGHEST = lax.Precision.HIGHEST
 NB = 128
 LOOK = 2
-STARTS = (0, 128, 384, 512)
+STARTS = (0, 128, 512)
 CHUNK = 64
 CHUNKS = 512 // CHUNK
 EARLY = (0, 6, 4, 2, 0, 0, 0, 1)

time: 25.8 us -> 25.7 us (level)
  no operation moved by 1% of the time
where the time goes in v5:
time: 25.7 us; the launch traced here: 25.4 us
  Pallas kernels  25.4 us (99%)
    pallas_call x1, Pallas kernels, per_device(): pl.pallas_call(functools.partial(gather_kernel, n), out_shape=[pltpu.VMEM...  23.2 us
    pallas_call x1, Pallas kernels, per_device(): pl.pallas_call(update_kernel, out_shape=pltpu.HBM((2048, NB), F32), in_sp...  2.16 us

profile of v5, /device:TPU:37, one launch (start us, length us, event | category | flops | bytes accessed | tf_op | source)
XLA Modules:
  0.0 25.4 jit_solution(7637471125680003798)
XLA Ops:
  0.0 23.2 %shard_map.17 = (f32[512,256]{1,0:T(8,128)S(1)}, f32[256,512]{1,0:T(8,128)S(1)}, f32[128,128]{1,0:T(8,128)S(1)}, f32[2048,128]{1,0:T(8,128)S(1)}) custom-call(f32[2048,128]{1,0:T(8,128)} %bitcast.4), custom_call_target="tpu_custom_call" | custom-call | tf_op jit(solution)/shard_map/pallas_call | solution.py:683
  23.2 2.2 %shard_map.18 = f32[2048,128]{1,0:T(8,128)} custom-call(f32[2048,128]{1,0:T(8,128)S(1)} %get-tuple-element.9.x, f32[512,256]{1,0:T(8,128)S(1)} %get-tuple-element.10.pr, f32[256,512]{1,0:T(8,128)S(1)} %get-tuple-element.11.pc, f32[128,128]{1,0:T(8,128)S(1)} %get-tuple-element.12.diag), custom_call_target="tpu_custom_call" | custom-call | tf_op jit(solution)/shard_map/pallas_call | solution.py:739

commit v6 on v5

--- a/solution.py
+++ b/solution.py
@@ -408,6 +408,7 @@
         w10[...] = dot_nn(l10, w0)
         arrive(lead.at[1], lead_recv.at[1])
         work[...] = lead[1] - dot_nt(l10, l10)
+        wown[:, 0] = inverse[0].reshape(n, 8, NB)
         enter()
         signal(go_plane, 1, 0)
 
@@ -521,7 +522,6 @@
             return carry
 
         lax.fori_loop(0, 2, block, 0)
-        wown[:, 0] = inverse[0].reshape(n, 8, NB)
         wown[:, 1] = -dot_nn(inverse[1], w10[...]).reshape(n, 8, NB)
         wown[:, 2] = inverse[1].reshape(n, 8, NB)
         for p in range(n):

time: 25.7 us -> 25.7 us (level)
  no operation moved by 1% of the time
where the time goes in v6:
time: 25.7 us; the launch traced here: 25.4 us
  Pallas kernels  25.4 us (99%)
    pallas_call x1, Pallas kernels, per_device(): pl.pallas_call(functools.partial(gather_kernel, n), out_shape=[pltpu.VMEM...  23.2 us
    pallas_call x1, Pallas kernels, per_device(): pl.pallas_call(update_kernel, out_shape=pltpu.HBM((2048, NB), F32), in_sp...  2.16 us

profile of v6, /device:TPU:37, one launch (start us, length us, event | category | flops | bytes accessed | tf_op | source)
XLA Modules:
  0.0 25.4 jit_solution(13370081185015504993)
XLA Ops:
  0.0 23.2 %shard_map.17 = (f32[512,256]{1,0:T(8,128)S(1)}, f32[256,512]{1,0:T(8,128)S(1)}, f32[128,128]{1,0:T(8,128)S(1)}, f32[2048,128]{1,0:T(8,128)S(1)}) custom-call(f32[2048,128]{1,0:T(8,128)} %bitcast.4), custom_call_target="tpu_custom_call" | custom-call | tf_op jit(solution)/shard_map/pallas_call | solution.py:683
  23.2 2.2 %shard_map.18 = f32[2048,128]{1,0:T(8,128)} custom-call(f32[2048,128]{1,0:T(8,128)S(1)} %get-tuple-element.9.x, f32[512,256]{1,0:T(8,128)S(1)} %get-tuple-element.10.pr, f32[256,512]{1,0:T(8,128)S(1)} %get-tuple-element.11.pc, f32[128,128]{1,0:T(8,128)S(1)} %get-tuple-element.12.diag), custom_call_target="tpu_custom_call" | custom-call | tf_op jit(solution)/shard_map/pallas_call | solution.py:739
